TPU v7x, 32 devices: a whole 2x2x4 slice. The times are simulated.
32 devices in a mesh: slab: 8 (over z, y), grp: 4 (over x, core).
Axes of the slice: x: 2, y: 2, z: 4, core: 2. Of those that a mesh axis runs over, the one named last changes fastest.
Arguments:
- positions: float32 [32, 16, 3, 128], P('slab', 'grp'), may hold values from 0 to 1
- sketch: bfloat16 [32, 16, 128, 256], P('slab', 'grp'), may hold values from -6 to 6
- counts: int32 [32, 16], P('slab', 'grp'), may hold values from 32 to 128, as said below
- neighbours: int32 [32, 16, 8], P('slab', 'grp'), may hold values from 0 to 8, as said below
Outputs:
- basis: bfloat16 [32, 16, 128, 256], P('slab', 'grp')
- factor: float32 [256, 256], replicated
Inputs may be any that keep to these rules, and one draw needn't show every extreme that they name: `counts`: the first block of every device's region of 4 x 4 blocks is full. `neighbours`: a code is 3 (dz + 1) + (dy + 1) for offsets dz, dy in -1, 0, 1; the codes of one block are distinct and always include 4 (the block itself); each block leaves out exactly one of its nine codes, and the lists are symmetric: block a lists block b if and only if block b lists block a; the left-out pairs lie inside aligned 2 x 2 squares of blocks.
All inputs are finite; a program needn't handle non-finite values.
Results may differ from a plain program's by a relative error of at most 0.017.
Values may be sent and summed in bfloat16 or wider, within the bound.
A program may use at most 64 MiB of HBM per device.

v0:
```python
import math
import jax
import jax.numpy as jnp
from jax import lax
from jax.sharding import PartitionSpec as P


def padded(shard, sides, width):
    for axis, dim in sides:
        count, length = (lax.axis_size(axis), shard.shape[dim])
        up = [(i, (i + 1) % count) for i in range(count)]
        down = [(j, i) for i, j in up]
        last = lax.slice_in_dim(shard, length - width, length, axis=dim)
        leading = lax.slice_in_dim(shard, 0, width, axis=dim)
        before = lax.ppermute(last, axis, up)
        after = lax.ppermute(leading, axis, down)
        shard = jnp.concatenate([before, shard, after], axis=dim)
    return shard


def kernel_tile(own_pos, other_pos, shift_z, shift_y):
    diff_z = other_pos[..., 0, None, :] + shift_z[..., None, None] - own_pos[..., 0, :, None]
    diff_y = other_pos[..., 1, None, :] + shift_y[..., None, None] - own_pos[..., 1, :, None]
    diff_x = other_pos[..., 2, None, :] - own_pos[..., 2, :, None]
    radius = jnp.sqrt(diff_z * diff_z + diff_y * diff_y + diff_x * diff_x)
    taper = jnp.maximum(1.0 - radius, 0.0)
    return taper**4 * (4.0 * radius + 1.0)


def on_device(positions, sketch, counts, neighbours):
    blocks_z, blocks_y, _, points = positions.shape
    columns = sketch.shape[3]
    live_mask = (
        lax.broadcasted_iota(jnp.int32, (blocks_z, blocks_y, points), 2) < counts[:, :, None]
    )
    masked = jnp.where(live_mask[..., None], sketch, jnp.zeros_like(sketch))
    wide_pos, wide_rows = (
        padded(positions.astype(jnp.bfloat16), (("slab", 0), ("grp", 1)), 1).astype(
            positions.dtype
        ),
        padded(masked, (("slab", 0), ("grp", 1)), 1),
    )
    pos_table = wide_pos.reshape(-1, 3, points)
    row_table = wide_rows.reshape(-1, points, columns)
    own_pos = positions.reshape(-1, 3, points)
    row_ids = lax.broadcasted_iota(jnp.int32, (blocks_z, blocks_y), 0)
    col_ids = lax.broadcasted_iota(jnp.int32, (blocks_z, blocks_y), 1)
    image = jnp.zeros((blocks_z * blocks_y, points, columns), jnp.float32)
    for slot_index in range(neighbours.shape[2]):
        offset_code = neighbours[:, :, slot_index]
        shift_z = offset_code // 3 - 1
        shift_y = offset_code % 3 - 1
        source_ids = ((row_ids + 1 + shift_z) * (blocks_y + 2) + col_ids + 1 + shift_y).reshape(-1)
        other_pos = jnp.take(pos_table, source_ids, axis=0)
        other_rows = jnp.take(row_table, source_ids, axis=0)
        weights = kernel_tile(
            own_pos,
            other_pos,
            shift_z.reshape(-1).astype(jnp.float32),
            shift_y.reshape(-1).astype(jnp.float32),
        ).astype(jnp.bfloat16)
        image = image + jnp.einsum(
            "bij,bjr->bir", weights, other_rows, preferred_element_type=jnp.float32
        )
    image = jnp.where(live_mask.reshape(-1, points)[..., None], image, jnp.zeros_like(image))
    flat_rows = image.reshape(-1, columns)
    gram_local = jnp.dot(
        flat_rows.T, flat_rows, preferred_element_type=jnp.float32, precision=lax.Precision.HIGHEST
    )
    gram_total = lax.psum(gram_local, ("slab", "grp"))
    lower_factor = jnp.linalg.cholesky(gram_total)
    solved = lax.linalg.triangular_solve(lower_factor, flat_rows.T, left_side=True, lower=True)
    total_rows = lax.axis_size("slab") * blocks_z * lax.axis_size("grp") * blocks_y * points
    scale_rows = math.sqrt(total_rows)
    basis = (
        (solved.T * scale_rows).reshape(blocks_z, blocks_y, points, columns).astype(jnp.bfloat16)
    )
    factor = lower_factor.T / scale_rows
    return (basis, factor)


def solution(mesh):
    placed = (
        P("slab", "grp", None, None),
        P("slab", "grp", None, None),
        P("slab", "grp"),
        P("slab", "grp", None),
    )
    return jax.shard_map(
        on_device,
        mesh=mesh,
        in_specs=placed,
        out_specs=(P("slab", "grp", None, None), P()),
        check_vma=False,
    )
```

profile of v0, /device:TPU:0, one launch (start us, length us, event | category | flops | bytes accessed | tf_op | source)
XLA Modules:
  0.0 279.9 jit_solution(16708323109046703102)
XLA Ops:
  7.2 0.7 convert_element_type.155
  8.0 3.0 %collective-permute-start = (bf16[1,4,3,128]{3,1,2,0:T(4,128)(2,1)S(1)}, bf16[1,4,3,128]{3,1,2,0:T(4,128)(2,1)S(1)}, u32[]{:S(2)}, u32[]{:S(2)}) collective-permute-start(bf16[1,4,3,128]{3,1,2,0:T(4,128)(2,1)S(1)} %get-tuple-element.121), channel_id=1, source_target_pairs={{0,4},{4,8},{8,12},{12,16},{16,20},{20,24},{24,28},{28,0},{1,5},{5... | collective-permute-start | bytes 9224 | tf_op jit(solution)/shard_map/ppermute | solution.py:15
  11.0 3.1 %collective-permute-start.1 = (bf16[1,4,3,128]{3,1,2,0:T(4,128)(2,1)S(1)}, bf16[1,4,3,128]{3,1,2,0:T(4,128)(2,1)S(1)}, u32[]{:S(2)}, u32[]{:S(2)}) collective-permute-start(bf16[1,4,3,128]{3,1,2,0:T(4,128)(2,1)S(1)} %get-tuple-element.122), channel_id=1, source_target_pairs={{4,0},{8,4},{12,8},{16,12},{20,16},{24,20},{28,24},{0,28},{5,1},{9... | collective-permute-start | bytes 9224 | tf_op jit(solution)/shard_map/ppermute | solution.py:16
  14.1 0.8 iota_compare_fusion.3
  14.9 1.5 broadcast_select_fusion
  16.5 4.7 %collective-permute-start.5 = (bf16[1,4,128,256]{3,2,1,0:T(8,128)(2,1)S(1)}, bf16[1,4,128,256]{3,2,1,0:T(8,128)(2,1)S(1)}, u32[]{:S(2)}, u32[]{:S(2)}) collective-permute-start(bf16[1,4,128,256]{3,2,1,0:T(8,128)(2,1)S(1)} %get-tuple-element.85), channel_id=1, source_target_pairs={{4,0},{8,4},{12,8},{16,12},{20,16},{24,20},{28,24},{0,28},{5,1},{9... | collective-permute-start | bytes 786440 | tf_op jit(solution)/shard_map/ppermute | solution.py:16
  21.3 0.7 fusion.121
  22.0 1.3 remainder_reduce_fusion
  26.2 1.7 collective-permute-start.3
  28.0 1.3 collective-permute-done.2
  29.4 0.6 gather_fusion.14
  30.0 0.6 gather_fusion.12
  30.6 0.6 gather_fusion.10
  31.2 0.6 gather_fusion.8
  31.7 0.6 gather_fusion.6
  32.3 0.6 gather_fusion.4
  33.8 0.7 slice_add_fusion.9
  34.4 0.7 slice_add_fusion.11
  35.1 0.6 gather_fusion.2
  35.7 0.6 gather_fusion
  36.6 1.7 collective-permute-start.6
  38.5 0.7 slice_add_fusion.13
  39.2 0.7 slice_add_fusion.15
  39.9 6.3 %collective-permute-done.6 = bf16[6,1,128,256]{3,2,1,0:T(8,128)(2,1)S(1)} collective-permute-done((bf16[6,1,128,256]{3,2,1,0:T(8,128)(2,1)S(1)}, bf16[6,1,128,256]{3,2,1,0:T(8,128)(2,1)S(1)}, u32[]{:S(2)}, u32[]{:S(2)}) %collective-permute-start.6) | collective-permute-done | bytes 393248 | tf_op jit(solution)/shard_map/ppermute | solution.py:15
  46.2 1.0 collective-permute-done.7
  47.2 1.4 pad_maximum_fusion
  48.6 0.6 gather_fusion.15
  49.2 1.7 gather_fusion.13
  50.9 1.7 gather_fusion.11
  52.6 1.7 gather_fusion.9
  54.3 1.7 gather_fusion.7
  56.0 1.7 gather_fusion.5
  57.8 1.8 gather_fusion.3
  59.6 1.8 gather_fusion.1
  61.4 2.4 fusion.5
  63.9 1.7 fusion.7
  65.6 1.7 fusion.9
  67.4 1.7 fusion.11
  69.2 1.7 fusion.13
  71.0 1.7 fusion.17
  72.7 1.7 fusion.15
  74.5 2.8 add_select_fusion
  77.2 4.2 %convolution_bitcast_fusion = f32[256,256]{0,1:T(8,128)} fusion(f32[16,128,256]{2,1,0:T(8,128)S(1)} %add_select_fusion), kind=kOutput, calls=%fused_computation.23 | convolution fusion | flops 1610612736 | bytes 2359296 | tf_op jit(solution)/shard_map/dot_general | solution.py:67
  81.4 122.8 %all-reduce.3.cloned.1.call-done = f32[256,256]{0,1:T(8,128)} async-done(((f32[256,256]{0,1:T(8,128)}), f32[256,256]{0,1:T(8,128)}) %all-reduce.3.cloned.1.call-update) | async-done | bytes 262160 | tf_op jit(solution)/shard_map/psum | solution.py:70
  204.2 1.1 copy.23
  205.3 1.0 fusion.107
  206.3 11.7 %cholesky.50 = f32[128,128]{1,0:T(8,128)S(1)} custom-call(f32[128,128]{1,0:T(8,128)S(1)} %cholesky.118), custom_call_target="Cholesky" | custom-call | tf_op jit(solution)/shard_map/jit(cholesky)/cholesky | solution.py:71
  218.1 0.6 compare_reduce_fusion.1
  218.7 9.8 %custom-call.14 = f32[1,128,128]{1,2,0:T(8,128)S(1)} custom-call(f32[1,128,128]{2,1,0:T(8,128)S(1)} %get-tuple-element.91), custom_call_target="InvertDiagBlocksLowerTriangular" | custom-call | tf_op jit(solution)/shard_map/jit(cholesky)/cholesky | solution.py:71
  228.6 0.2 constant_dynamic-update-slice_fusion.1
  228.8 0.3 convolution_subtract_fusion.1
  229.0 11.9 %cholesky.105 = f32[128,128]{1,0:T(8,128)S(1)} custom-call(f32[128,128]{1,0:T(8,128)S(1)} %convolution_subtract_fusion.1), custom_call_target="Cholesky" | custom-call | tf_op jit(solution)/shard_map/jit(cholesky)/cholesky | solution.py:71
  241.0 0.7 compare_reduce_fusion
  243.0 0.8 copy.25
  243.9 4.0 %while.1 = (s32[]{:T(128)}, f32[256,256]{1,0:T(8,128)S(1)}, s32[2,2]{1,0:T(2,128)S(1)}, f32[2,128,128]{2,1,0:T(8,128)S(1)}, s32[]{:T(128)}) while((s32[]{:T(128)}, f32[256,256]{1,0:T(8,128)S(1)}, s32[2,2]{1,0:T(2,128)S(1)}, f32[2,128,128]{2,1,0:T(8,128)S(1)}, s32[]{:T(128)}) %tuple.117), condition=%wide.while_cond, body=%wide.while_body.sunk | while | flops 2 | bytes 131189 | solution.py:72
  243.9 0.6 fusion.205
  244.6 1.3 bitcast_dynamic-update-slice_fusion.2
  246.0 0.6 fusion.205
  246.6 1.3 bitcast_dynamic-update-slice_fusion.2
  247.9 19.7 %custom-call.15 = f32[2,128,128]{1,2,0:T(8,128)S(1)} custom-call(f32[2,128,128]{2,1,0:T(8,128)S(1)} %get-tuple-element.11), custom_call_target="InvertDiagBlocksLowerTriangular" | custom-call | tf_op jit(solution)/shard_map/triangular_solve | solution.py:72
  267.6 1.1 fusion.2
  268.7 1.8 convolution_subtract_fusion
  270.5 1.1 fusion.110
  271.8 1.3 copy.29
  (174 shorter events, 4.6 us)
Async XLA Ops:
  7.2 14.1 %copy-start.9 = (f32[4,4,3,128]{3,1,2,0:T(4,128)S(1)}, f32[4,4,3,128]{3,1,2,0:T(4,128)}, u32[]{:S(2)}) copy-start(f32[4,4,3,128]{3,1,2,0:T(4,128)} %param.8) | copy-start | bytes 73732
  7.2 14.0 %copy-start.20 = (s32[4,4]{1,0:T(4,128)S(1)}, s32[4,4]{1,0:T(4,128)}, u32[]{:S(2)}) copy-start(s32[4,4]{1,0:T(4,128)} %param.10) | copy-start | bytes 196
  7.2 14.1 %copy-start = (s32[4,4,8]{2,1,0:T(4,128)S(1)}, s32[4,4,8]{2,1,0:T(4,128)}, u32[]{:S(2)}) copy-start(s32[4,4,8]{2,1,0:T(4,128)} %param.11) | copy-start | bytes 1540
  7.2 197.0 %all-reduce.3.cloned.1.call-start = ((), (), s32[]{:S(2)}) async-start(), calls=%async_computation | async-start | bytes 524288 | tf_op jit(solution)/shard_map/psum | solution.py:70
  8.0 18.1 %collective-permute-start = (bf16[1,4,3,128]{3,1,2,0:T(4,128)(2,1)S(1)}, bf16[1,4,3,128]{3,1,2,0:T(4,128)(2,1)S(1)}, u32[]{:S(2)}, u32[]{:S(2)}) collective-permute-start(bf16[1,4,3,128]{3,1,2,0:T(4,128)(2,1)S(1)} %get-tuple-element.121), channel_id=1, source_target_pairs={{0,4},{4,8},{8,12},{12,16},{16,20},{20,24},{24,28},{28,0},{1,5},{5... | collective-permute-start | bytes 9224 | tf_op jit(solution)/shard_map/ppermute | solution.py:15
  11.0 15.1 %collective-permute-start.1 = (bf16[1,4,3,128]{3,1,2,0:T(4,128)(2,1)S(1)}, bf16[1,4,3,128]{3,1,2,0:T(4,128)(2,1)S(1)}, u32[]{:S(2)}, u32[]{:S(2)}) collective-permute-start(bf16[1,4,3,128]{3,1,2,0:T(4,128)(2,1)S(1)} %get-tuple-element.122), channel_id=1, source_target_pairs={{4,0},{8,4},{12,8},{16,12},{20,16},{24,20},{28,24},{0,28},{5,1},{9... | collective-permute-start | bytes 9224 | tf_op jit(solution)/shard_map/ppermute | solution.py:16
  16.4 20.1 %collective-permute-start.4 = (bf16[1,4,128,256]{3,2,1,0:T(8,128)(2,1)S(1)}, bf16[1,4,128,256]{3,2,1,0:T(8,128)(2,1)S(1)}, u32[]{:S(2)}, u32[]{:S(2)}) collective-permute-start(bf16[1,4,128,256]{3,2,1,0:T(8,128)(2,1)S(1)} %get-tuple-element.84), channel_id=1, source_target_pairs={{0,4},{4,8},{8,12},{12,16},{16,20},{20,24},{24,28},{28,0},{1,5},{5... | collective-permute-start | bytes 786440 | tf_op jit(solution)/shard_map/ppermute | solution.py:15
  16.5 20.0 %collective-permute-start.5 = (bf16[1,4,128,256]{3,2,1,0:T(8,128)(2,1)S(1)}, bf16[1,4,128,256]{3,2,1,0:T(8,128)(2,1)S(1)}, u32[]{:S(2)}, u32[]{:S(2)}) collective-permute-start(bf16[1,4,128,256]{3,2,1,0:T(8,128)(2,1)S(1)} %get-tuple-element.85), channel_id=1, source_target_pairs={{4,0},{8,4},{12,8},{16,12},{20,16},{24,20},{28,24},{0,28},{5,1},{9... | collective-permute-start | bytes 786440 | tf_op jit(solution)/shard_map/ppermute | solution.py:16
  25.8 7.3 %copy-start.28 = (pred[16]{0:T(512)(128)(4,1)}, pred[16]{0:T(512)(128)(4,1)S(1)}, u32[]{:S(2)}) copy-start(pred[16]{0:T(512)(128)(4,1)S(1)} %get-tuple-element.50) | copy-start | bytes 52
  25.9 7.9 %copy-start.34 = (pred[16]{0:T(512)(128)(4,1)}, pred[16]{0:T(512)(128)(4,1)S(1)}, u32[]{:S(2)}) copy-start(pred[16]{0:T(512)(128)(4,1)S(1)} %get-tuple-element.131) | copy-start | bytes 52
  25.9 7.9 %copy-start.36 = (pred[16]{0:T(512)(128)(4,1)}, pred[16]{0:T(512)(128)(4,1)S(1)}, u32[]{:S(2)}) copy-start(pred[16]{0:T(512)(128)(4,1)S(1)} %get-tuple-element.129) | copy-start | bytes 52
  25.9 7.9 %copy-start.38 = (pred[16]{0:T(512)(128)(4,1)}, pred[16]{0:T(512)(128)(4,1)S(1)}, u32[]{:S(2)}) copy-start(pred[16]{0:T(512)(128)(4,1)S(1)} %get-tuple-element.127) | copy-start | bytes 52
  25.9 7.9 %copy-start.40 = (pred[16]{0:T(512)(128)(4,1)}, pred[16]{0:T(512)(128)(4,1)S(1)}, u32[]{:S(2)}) copy-start(pred[16]{0:T(512)(128)(4,1)S(1)} %get-tuple-element.125) | copy-start | bytes 52
  25.9 10.4 %copy-start.42 = (pred[16]{0:T(512)(128)(4,1)}, pred[16]{0:T(512)(128)(4,1)S(1)}, u32[]{:S(2)}) copy-start(pred[16]{0:T(512)(128)(4,1)S(1)} %get-tuple-element.123) | copy-start | bytes 52
  25.9 13.3 %copy-start.30 = (pred[16]{0:T(512)(128)(4,1)}, pred[16]{0:T(512)(128)(4,1)S(1)}, u32[]{:S(2)}) copy-start(pred[16]{0:T(512)(128)(4,1)S(1)} %get-tuple-element.133) | copy-start | bytes 52
  25.9 13.3 %copy-start.32 = (pred[16]{0:T(512)(128)(4,1)}, pred[16]{0:T(512)(128)(4,1)S(1)}, u32[]{:S(2)}) copy-start(pred[16]{0:T(512)(128)(4,1)S(1)} %get-tuple-element.135) | copy-start | bytes 52
  25.9 7.1 %copy-start.21 = (s32[1024]{0:T(1024)}, s32[1024]{0:T(1024)S(1)}, u32[]{:S(2)}) copy-start(s32[1024]{0:T(1024)S(1)} %pad_clamp_fusion.1) | copy-start | bytes 12292
  26.0 7.1 %copy-start.22 = (s32[1024]{0:T(1024)}, s32[1024]{0:T(1024)S(1)}, u32[]{:S(2)}) copy-start(s32[1024]{0:T(1024)S(1)} %pad_clamp_fusion.2) | copy-start | bytes 12292
  26.0 7.2 %copy-start.23 = (s32[1024]{0:T(1024)}, s32[1024]{0:T(1024)S(1)}, u32[]{:S(2)}) copy-start(s32[1024]{0:T(1024)S(1)} %pad_clamp_fusion.3) | copy-start | bytes 12292
  26.0 7.1 %copy-start.24 = (s32[1024]{0:T(1024)}, s32[1024]{0:T(1024)S(1)}, u32[]{:S(2)}) copy-start(s32[1024]{0:T(1024)S(1)} %pad_clamp_fusion.4) | copy-start | bytes 12292
  26.0 7.1 %copy-start.25 = (s32[1024]{0:T(1024)}, s32[1024]{0:T(1024)S(1)}, u32[]{:S(2)}) copy-start(s32[1024]{0:T(1024)S(1)} %pad_clamp_fusion.5) | copy-start | bytes 12292
  26.1 10.3 %copy-start.26 = (s32[1024]{0:T(1024)}, s32[1024]{0:T(1024)S(1)}, u32[]{:S(2)}) copy-start(s32[1024]{0:T(1024)S(1)} %pad_clamp_fusion.6) | copy-start | bytes 12292
  26.2 3.1 %collective-permute-start.2 = (bf16[6,1,3,128]{3,1,2,0:T(2,128)(2,1)S(1)}, bf16[6,1,3,128]{3,1,2,0:T(2,128)(2,1)S(1)}, u32[]{:S(2)}, u32[]{:S(2)}) collective-permute-start(bf16[6,1,3,128]{3,1,2,0:T(2,128)(2,1)S(1)} %get-tuple-element.119), channel_id=1, source_target_pairs={{0,1},{1,2},{2,3},{3,0},{4,5},{5,6},{6,7},{7,4},{8,9},{9,10},{10,1... | collective-permute-start | bytes 13832 | tf_op jit(solution)/shard_map/ppermute | solution.py:15
  26.2 3.1 %collective-permute-start.3 = (bf16[6,1,3,128]{3,1,2,0:T(2,128)(2,1)S(1)}, bf16[6,1,3,128]{3,1,2,0:T(2,128)(2,1)S(1)}, u32[]{:S(2)}, u32[]{:S(2)}) collective-permute-start(bf16[6,1,3,128]{3,1,2,0:T(2,128)(2,1)S(1)} %get-tuple-element.120), channel_id=1, source_target_pairs={{1,0},{2,1},{3,2},{0,3},{5,4},{6,5},{7,6},{4,7},{9,8},{10,9},{11,1... | collective-permute-start | bytes 13832 | tf_op jit(solution)/shard_map/ppermute | solution.py:16
  28.0 8.4 %copy-start.27 = (s32[1024]{0:T(1024)}, s32[1024]{0:T(1024)S(1)}, u32[]{:S(2)}) copy-start(s32[1024]{0:T(1024)S(1)} %pad_clamp_fusion.7) | copy-start | bytes 12292
  36.5 9.7 %copy-start.1 = (bf16[1,4,128,256]{3,2,1,0:T(8,128)(2,1)}, bf16[1,4,128,256]{3,2,1,0:T(8,128)(2,1)S(1)}, u32[]{:S(2)}) copy-start(bf16[1,4,128,256]{3,2,1,0:T(8,128)(2,1)S(1)} %collective-permute-done.4) | copy-start | bytes 786436
  36.5 9.7 %copy-start.2 = (bf16[1,4,128,256]{3,2,1,0:T(8,128)(2,1)}, bf16[1,4,128,256]{3,2,1,0:T(8,128)(2,1)S(1)}, u32[]{:S(2)}) copy-start(bf16[1,4,128,256]{3,2,1,0:T(8,128)(2,1)S(1)} %collective-permute-done.5) | copy-start | bytes 786436
  36.6 9.6 %collective-permute-start.6 = (bf16[6,1,128,256]{3,2,1,0:T(8,128)(2,1)S(1)}, bf16[6,1,128,256]{3,2,1,0:T(8,128)(2,1)S(1)}, u32[]{:S(2)}, u32[]{:S(2)}) collective-permute-start(bf16[6,1,128,256]{3,2,1,0:T(8,128)(2,1)S(1)} %get-tuple-element.82), channel_id=1, source_target_pairs={{0,1},{1,2},{2,3},{3,0},{4,5},{5,6},{6,7},{7,4},{8,9},{9,10},{10,1... | collective-permute-start | bytes 1179656 | tf_op jit(solution)/shard_map/ppermute | solution.py:15
  38.3 8.9 %collective-permute-start.7 = (bf16[6,1,128,256]{3,2,1,0:T(8,128)(2,1)S(1)}, bf16[6,1,128,256]{3,2,1,0:T(8,128)(2,1)S(1)}, u32[]{:S(2)}, u32[]{:S(2)}) collective-permute-start(bf16[6,1,128,256]{3,2,1,0:T(8,128)(2,1)S(1)} %get-tuple-element.83), channel_id=1, source_target_pairs={{1,0},{2,1},{3,2},{0,3},{5,4},{6,5},{7,6},{4,7},{9,8},{10,9},{11,1... | collective-permute-start | bytes 1179656 | tf_op jit(solution)/shard_map/ppermute | solution.py:16
  57.8 3.6 %copy-start.43 = (pred[16]{0:T(512)(128)(4,1)S(1)}, pred[16]{0:T(512)(128)(4,1)}, u32[]{:S(2)}) copy-start(pred[16]{0:T(512)(128)(4,1)} %copy-done.42) | copy-start | bytes 52
  61.4 2.4 copy-start.8
  61.4 2.4 copy-start.41
  63.8 1.7 copy-start.7
  63.8 1.7 copy-start.39
  65.6 1.7 copy-start.6
  65.6 1.7 copy-start.10
  65.6 1.7 copy-start.37
  67.3 1.8 copy-start.5
  67.3 1.8 copy-start.11
  67.4 1.8 copy-start.12
  67.4 1.8 copy-start.13
  67.4 1.8 copy-start.35
  69.1 1.8 copy-start.4
  69.1 1.8 copy-start.17
  69.2 1.8 copy-start.18
  69.2 1.8 copy-start.19
  69.2 1.8 copy-start.33
  70.9 1.8 copy-start.3
  70.9 1.8 copy-start.14
  71.0 1.8 copy-start.15
  71.0 1.8 copy-start.16
  71.0 1.8 copy-start.31
  72.7 1.7 copy-start.29
Sparse Core Ops, SparseCore 0:
  81.5 122.6 all-reduce.2
where the time goes:
time: 280 us
  waiting for transfers between devices  131 us (47%)
  other arithmetic  66.1 us (24%)
  local copies, waits for them, and re-layouts  27.4 us (10%)
  matrix products  24 us (9%)
  between operations  16.4 us (6%)
  starting transfers between devices  14.6 us (5%)
    psum x1, waiting for transfers between devices, on_device(): gram_total = lax.psum(gram_local, ('slab', 'grp'))  123 us
    another operation x7, other arithmetic, on_device(): lower_factor = jnp.linalg.cholesky(gram_total)  34.8 us
    another operation x2, other arithmetic, on_device(): lax.linalg.triangular_solve(lower_factor, flat_rows.T, left_side=True, lo...  19.7 us
    dot_general x8, matrix products, on_device(): jnp.einsum('bij,bjr->bir', weights, other_rows, preferred_element_type=jn...  15.4 us
    gather x8, local copies, waits for them, and re-layouts, on_device(): other_rows = jnp.take(row_table, source_ids, axis=0)  12.8 us
    ppermute x4, starting transfers between devices, padded(): after = lax.ppermute(leading, axis, down)  9.73 us
    ppermute x4, waiting for transfers between devices, padded(): before = lax.ppermute(last, axis, up)  7.6 us
  transfers between devices with their start and end apart: 9, of which 4 were waited for; matrix products, arithmetic and copies ran while one was open for 5% of the time, Pallas kernels for 0%

commit v1 on v0

--- a/solution.py
+++ b/solution.py
@@ -67,7 +67,7 @@
     gram_local = jnp.dot(
         flat_rows.T, flat_rows, preferred_element_type=jnp.float32, precision=lax.Precision.HIGHEST
     )
-    gram_total = lax.psum(gram_local, ("slab", "grp"))
+    gram_total = jnp.sum(lax.all_gather(gram_local, ("slab", "grp")), axis=0)
     lower_factor = jnp.linalg.cholesky(gram_total)
     solved = lax.linalg.triangular_solve(lower_factor, flat_rows.T, left_side=True, lower=True)
     total_rows = lax.axis_size("slab") * blocks_z * lax.axis_size("grp") * blocks_y * points

time: 280 us -> 234 us (0.84)
  waiting for transfers between devices: 131 us -> 81.9 us
  other arithmetic: 66.1 us -> 69.1 us
    psum x1 -> x0, waiting for transfers between devices: 123 us -> none  [on_device(): gram_total = lax.psum(gram_local, ('slab', 'grp'))]
    all_gather x0 -> x1, waiting for transfers between devices: none -> 73.5 us  [on_device(): gram_total = jnp.sum(lax.all_gather(gram_local, ('slab', 'grp')), axis=0)]
    reduce_sum x0 -> x1, other arithmetic: none -> 3.93 us  [on_device(): gram_total = jnp.sum(lax.all_gather(gram_local, ('slab', 'grp')), axis=0)]
  transfers between devices with their start and end apart: 9 -> 9, of which waited for: 4 -> 4; matrix products, arithmetic and copies ran while one was open for 5% -> 7% of each run, Pallas kernels for 0% -> 0%
where the time goes in v1:
time: 234 us; the launch traced here: 233 us
  waiting for transfers between devices  81.9 us (35%)
  other arithmetic  69.1 us (30%)
  local copies, waits for them, and re-layouts  28.2 us (12%)
  matrix products  23 us (10%)
  between operations  16.4 us (7%)
  starting transfers between devices  14.8 us (6%)
    all_gather x1, waiting for transfers between devices, on_device(): gram_total = jnp.sum(lax.all_gather(gram_local, ('slab', 'grp')), axis=0)  73.5 us
    another operation x7, other arithmetic, on_device(): lower_factor = jnp.linalg.cholesky(gram_total)  34.6 us
    another operation x2, other arithmetic, on_device(): lax.linalg.triangular_solve(lower_factor, flat_rows.T, left_side=True, lo...  19.9 us
    dot_general x8, matrix products, on_device(): jnp.einsum('bij,bjr->bir', weights, other_rows, preferred_element_type=jn...  15.2 us
    gather x8, local copies, waits for them, and re-layouts, on_device(): other_rows = jnp.take(row_table, source_ids, axis=0)  12.8 us
    ppermute x4, starting transfers between devices, padded(): after = lax.ppermute(leading, axis, down)  9.91 us
    ppermute x4, waiting for transfers between devices, padded(): before = lax.ppermute(last, axis, up)  7.23 us
    ppermute x4, starting transfers between devices, padded(): before = lax.ppermute(last, axis, up)  4.86 us
  transfers between devices with their start and end apart: 9, of which 4 were waited for; matrix products, arithmetic and copies ran while one was open for 7% of the time, Pallas kernels for 0%

profile of v1, /device:TPU:0, one launch (start us, length us, event | category | flops | bytes accessed | tf_op | source)
XLA Modules:
  0.0 233.4 jit_solution(14034967263935298063)
XLA Ops:
  7.2 0.7 convert_element_type.155
  8.0 3.0 %collective-permute-start = (bf16[1,4,3,128]{3,1,2,0:T(4,128)(2,1)S(1)}, bf16[1,4,3,128]{3,1,2,0:T(4,128)(2,1)S(1)}, u32[]{:S(2)}, u32[]{:S(2)}) collective-permute-start(bf16[1,4,3,128]{3,1,2,0:T(4,128)(2,1)S(1)} %get-tuple-element.123), channel_id=1, source_target_pairs={{0,4},{4,8},{8,12},{12,16},{16,20},{20,24},{24,28},{28,0},{1,5},{5... | collective-permute-start | bytes 9224 | tf_op jit(solution)/shard_map/ppermute | solution.py:15
  11.0 3.1 %collective-permute-start.1 = (bf16[1,4,3,128]{3,1,2,0:T(4,128)(2,1)S(1)}, bf16[1,4,3,128]{3,1,2,0:T(4,128)(2,1)S(1)}, u32[]{:S(2)}, u32[]{:S(2)}) collective-permute-start(bf16[1,4,3,128]{3,1,2,0:T(4,128)(2,1)S(1)} %get-tuple-element.124), channel_id=1, source_target_pairs={{4,0},{8,4},{12,8},{16,12},{20,16},{24,20},{28,24},{0,28},{5,1},{9... | collective-permute-start | bytes 9224 | tf_op jit(solution)/shard_map/ppermute | solution.py:16
  14.1 0.8 iota_compare_fusion.3
  14.9 1.5 broadcast_select_fusion
  16.5 4.7 %collective-permute-start.5 = (bf16[1,4,128,256]{3,2,1,0:T(8,128)(2,1)S(1)}, bf16[1,4,128,256]{3,2,1,0:T(8,128)(2,1)S(1)}, u32[]{:S(2)}, u32[]{:S(2)}) collective-permute-start(bf16[1,4,128,256]{3,2,1,0:T(8,128)(2,1)S(1)} %get-tuple-element.87), channel_id=1, source_target_pairs={{4,0},{8,4},{12,8},{16,12},{20,16},{24,20},{28,24},{0,28},{5,1},{9... | collective-permute-start | bytes 786440 | tf_op jit(solution)/shard_map/ppermute | solution.py:16
  21.3 0.7 fusion.121
  22.0 1.3 remainder_reduce_fusion
  26.2 1.7 collective-permute-start.3
  28.0 1.3 collective-permute-done.2
  29.4 0.6 gather_fusion.14
  30.0 0.6 gather_fusion.12
  30.6 0.6 gather_fusion.10
  31.2 0.6 gather_fusion.8
  31.8 0.6 gather_fusion.6
  32.3 0.6 gather_fusion.4
  33.8 0.7 slice_add_fusion.9
  34.4 0.7 slice_add_fusion.11
  35.2 0.6 gather_fusion.2
  35.7 0.6 gather_fusion
  36.6 1.7 collective-permute-start.6
  38.3 0.4 collective-permute-start.7
  38.7 0.7 slice_add_fusion.13
  39.4 0.7 slice_add_fusion.15
  40.1 5.9 %collective-permute-done.6 = bf16[6,1,128,256]{3,2,1,0:T(8,128)(2,1)S(1)} collective-permute-done((bf16[6,1,128,256]{3,2,1,0:T(8,128)(2,1)S(1)}, bf16[6,1,128,256]{3,2,1,0:T(8,128)(2,1)S(1)}, u32[]{:S(2)}, u32[]{:S(2)}) %collective-permute-start.6) | collective-permute-done | bytes 393248 | tf_op jit(solution)/shard_map/ppermute | solution.py:15
  46.0 1.2 collective-permute-done.7
  47.2 1.4 pad_maximum_fusion
  48.5 0.6 gather_fusion.15
  49.2 1.7 gather_fusion.13
  50.9 1.7 gather_fusion.11
  52.6 1.7 gather_fusion.9
  54.3 1.7 gather_fusion.7
  56.0 1.7 gather_fusion.5
  57.8 1.8 gather_fusion.3
  59.6 1.7 gather_fusion.1
  61.4 2.4 %fusion.5 = f32[16,128,256]{2,1,0:T(8,128)S(1)} fusion(bf16[16,128,256]{2,1,0:T(8,128)(2,1)} %gather_fusion.13, pred[16]{0:T(512)(128)(4,1)S(1)} %copy-done.44, f32[16,128]{1,0:T(8,128)S(1)} %bitcast.102, f32[16,128]{1,0:T(8,128)S(1)} %bitcast.103, f32[16,128]{1,0:T(8,128)S(1)} %bitcast.101, f32[16,128]{1,0:T(8,128)S(1)} %get-tuple-element.119, ...), kind=kOutput, calls=%fused_computation.29 | convolution fusion | flops 138936320 | bytes 3194896 | tf_op jit(solution)/shard_map/bij,bjr->bir/dot_general | solution.py:62
  63.8 1.7 fusion.7
  65.6 1.7 fusion.9
  67.4 1.7 fusion.11
  69.2 1.7 fusion.13
  71.0 1.7 fusion.17
  72.7 1.7 fusion.15
  74.4 2.6 %add_select_fusion = f32[16,128,256]{2,1,0:T(8,128)S(1)} fusion(f32[16,128,256]{2,1,0:T(8,128)S(1)} %fusion.5, f32[16,128,256]{2,1,0:T(8,128)S(1)} %fusion.7, f32[16,128,256]{2,1,0:T(8,128)S(1)} %fusion.9, f32[16,128,256]{2,1,0:T(8,128)S(1)} %fusion.11, f32[16,128,256]{2,1,0:T(8,128)S(1)} %fusion.13, f32[16,128,256]{2,1,0:T(8,128)S(1)} %fusion.17, ...), kind=kOutput, calls=%fused_computation.22 | convolution fusion | flops 143130624 | bytes 17877008 | tf_op jit(solution)/shard_map/bij,bjr->bir/dot_general | solution.py:62
  77.0 4.2 %convolution_bitcast_fusion = f32[256,256]{1,0:T(8,128)} fusion(f32[16,128,256]{2,1,0:T(8,128)S(1)} %add_select_fusion), kind=kOutput, calls=%fused_computation.23 | convolution fusion | flops 1610612736 | bytes 2359296 | tf_op jit(solution)/shard_map/dot_general | solution.py:67
  81.3 1.9 copy.36
  83.1 73.5 %all-gather.3.cloned.1.call-done = f32[8192,256]{1,0:T(8,128)} async-done(((f32[256,256]{1,0:T(8,128)}), f32[8192,256]{1,0:T(8,128)}) %all-gather.3.cloned.1.call-update) | async-done | bytes 8388624 | tf_op jit(solution)/shard_map/all_gather | solution.py:70
  156.6 3.9 %reduce_sum.9 = f32[256,256]{1,0:T(8,128)S(1)} reduce(f32[32,256,256]{2,1,0:T(8,128)} %bitcast.87, f32[]{:T(128)} %constant.182.clone.1), dimensions={0}, to_apply=%region_0.3 | reduce | flops 2031616 | bytes 8650756 | tf_op jit(solution)/shard_map/reduce_sum | solution.py:70
  160.7 11.7 %cholesky.50 = f32[128,128]{1,0:T(8,128)S(1)} custom-call(f32[128,128]{1,0:T(8,128)S(1)} %cholesky.118), custom_call_target="Cholesky" | custom-call | tf_op jit(solution)/shard_map/jit(cholesky)/cholesky | solution.py:71
  172.5 0.6 compare_reduce_fusion.1
  173.1 9.8 %custom-call.14 = f32[1,128,128]{1,2,0:T(8,128)S(1)} custom-call(f32[1,128,128]{2,1,0:T(8,128)S(1)} %get-tuple-element.93), custom_call_target="InvertDiagBlocksLowerTriangular" | custom-call | tf_op jit(solution)/shard_map/jit(cholesky)/cholesky | solution.py:71
  183.1 0.3 convolution_subtract_fusion.1
  183.4 11.7 %cholesky.105 = f32[128,128]{1,0:T(8,128)S(1)} custom-call(f32[128,128]{1,0:T(8,128)S(1)} %convolution_subtract_fusion.1), custom_call_target="Cholesky" | custom-call | tf_op jit(solution)/shard_map/jit(cholesky)/cholesky | solution.py:71
  195.2 0.7 compare_reduce_fusion
  197.1 0.8 copy.38
  198.0 3.9 %while.1 = (s32[]{:T(128)}, f32[256,256]{1,0:T(8,128)S(1)}, s32[2,2]{1,0:T(2,128)S(1)}, f32[2,128,128]{2,1,0:T(8,128)S(1)}, s32[]{:T(128)}) while((s32[]{:T(128)}, f32[256,256]{1,0:T(8,128)S(1)}, s32[2,2]{1,0:T(2,128)S(1)}, f32[2,128,128]{2,1,0:T(8,128)S(1)}, s32[]{:T(128)}) %tuple.118), condition=%wide.while_cond, body=%wide.while_body.sunk | while | flops 2 | bytes 131189 | solution.py:72
  198.1 0.6 fusion.205
  198.7 1.3 bitcast_dynamic-update-slice_fusion.2
  200.0 0.6 fusion.205
  200.6 1.3 bitcast_dynamic-update-slice_fusion.2
  202.0 19.9 %custom-call.15 = f32[2,128,128]{1,2,0:T(8,128)S(1)} custom-call(f32[2,128,128]{2,1,0:T(8,128)S(1)} %get-tuple-element.11), custom_call_target="InvertDiagBlocksLowerTriangular" | custom-call | tf_op jit(solution)/shard_map/triangular_solve | solution.py:72
  221.9 1.1 fusion.2
  223.0 1.0 convolution_subtract_fusion
  224.0 1.1 fusion.110
  225.2 1.3 copy.40
  (178 shorter events, 4.8 us)
Async XLA Ops:
  7.2 14.1 %copy-start.10 = (f32[4,4,3,128]{3,1,2,0:T(4,128)S(1)}, f32[4,4,3,128]{3,1,2,0:T(4,128)}, u32[]{:S(2)}) copy-start(f32[4,4,3,128]{3,1,2,0:T(4,128)} %param.8) | copy-start | bytes 73732
  7.2 14.0 %copy-start.21 = (s32[4,4]{1,0:T(4,128)S(1)}, s32[4,4]{1,0:T(4,128)}, u32[]{:S(2)}) copy-start(s32[4,4]{1,0:T(4,128)} %param.10) | copy-start | bytes 196
  7.2 14.1 %copy-start.1 = (s32[4,4,8]{2,1,0:T(4,128)S(1)}, s32[4,4,8]{2,1,0:T(4,128)}, u32[]{:S(2)}) copy-start(s32[4,4,8]{2,1,0:T(4,128)} %param.11) | copy-start | bytes 1540
  7.2 149.4 %all-gather.3.cloned.1.call-start = ((), (), s32[]{:S(2)}) async-start(), calls=%async_computation | async-start | bytes 8650752 | tf_op jit(solution)/shard_map/all_gather | solution.py:70
  8.0 18.1 %collective-permute-start = (bf16[1,4,3,128]{3,1,2,0:T(4,128)(2,1)S(1)}, bf16[1,4,3,128]{3,1,2,0:T(4,128)(2,1)S(1)}, u32[]{:S(2)}, u32[]{:S(2)}) collective-permute-start(bf16[1,4,3,128]{3,1,2,0:T(4,128)(2,1)S(1)} %get-tuple-element.123), channel_id=1, source_target_pairs={{0,4},{4,8},{8,12},{12,16},{16,20},{20,24},{24,28},{28,0},{1,5},{5... | collective-permute-start | bytes 9224 | tf_op jit(solution)/shard_map/ppermute | solution.py:15
  11.0 15.1 %collective-permute-start.1 = (bf16[1,4,3,128]{3,1,2,0:T(4,128)(2,1)S(1)}, bf16[1,4,3,128]{3,1,2,0:T(4,128)(2,1)S(1)}, u32[]{:S(2)}, u32[]{:S(2)}) collective-permute-start(bf16[1,4,3,128]{3,1,2,0:T(4,128)(2,1)S(1)} %get-tuple-element.124), channel_id=1, source_target_pairs={{4,0},{8,4},{12,8},{16,12},{20,16},{24,20},{28,24},{0,28},{5,1},{9... | collective-permute-start | bytes 9224 | tf_op jit(solution)/shard_map/ppermute | solution.py:16
  16.4 20.0 %collective-permute-start.4 = (bf16[1,4,128,256]{3,2,1,0:T(8,128)(2,1)S(1)}, bf16[1,4,128,256]{3,2,1,0:T(8,128)(2,1)S(1)}, u32[]{:S(2)}, u32[]{:S(2)}) collective-permute-start(bf16[1,4,128,256]{3,2,1,0:T(8,128)(2,1)S(1)} %get-tuple-element.86), channel_id=1, source_target_pairs={{0,4},{4,8},{8,12},{12,16},{16,20},{20,24},{24,28},{28,0},{1,5},{5... | collective-permute-start | bytes 786440 | tf_op jit(solution)/shard_map/ppermute | solution.py:15
  16.5 20.0 %collective-permute-start.5 = (bf16[1,4,128,256]{3,2,1,0:T(8,128)(2,1)S(1)}, bf16[1,4,128,256]{3,2,1,0:T(8,128)(2,1)S(1)}, u32[]{:S(2)}, u32[]{:S(2)}) collective-permute-start(bf16[1,4,128,256]{3,2,1,0:T(8,128)(2,1)S(1)} %get-tuple-element.87), channel_id=1, source_target_pairs={{4,0},{8,4},{12,8},{16,12},{20,16},{24,20},{28,24},{0,28},{5,1},{9... | collective-permute-start | bytes 786440 | tf_op jit(solution)/shard_map/ppermute | solution.py:16
  25.8 7.3 %copy-start.29 = (pred[16]{0:T(512)(128)(4,1)}, pred[16]{0:T(512)(128)(4,1)S(1)}, u32[]{:S(2)}) copy-start(pred[16]{0:T(512)(128)(4,1)S(1)} %get-tuple-element.52) | copy-start | bytes 52
  25.9 7.3 %copy-start.43 = (pred[16]{0:T(512)(128)(4,1)}, pred[16]{0:T(512)(128)(4,1)S(1)}, u32[]{:S(2)}) copy-start(pred[16]{0:T(512)(128)(4,1)S(1)} %get-tuple-element.125) | copy-start | bytes 52
  25.9 7.9 %copy-start.35 = (pred[16]{0:T(512)(128)(4,1)}, pred[16]{0:T(512)(128)(4,1)S(1)}, u32[]{:S(2)}) copy-start(pred[16]{0:T(512)(128)(4,1)S(1)} %get-tuple-element.133) | copy-start | bytes 52
  25.9 7.9 %copy-start.37 = (pred[16]{0:T(512)(128)(4,1)}, pred[16]{0:T(512)(128)(4,1)S(1)}, u32[]{:S(2)}) copy-start(pred[16]{0:T(512)(128)(4,1)S(1)} %get-tuple-element.131) | copy-start | bytes 52
  25.9 7.9 %copy-start.39 = (pred[16]{0:T(512)(128)(4,1)}, pred[16]{0:T(512)(128)(4,1)S(1)}, u32[]{:S(2)}) copy-start(pred[16]{0:T(512)(128)(4,1)S(1)} %get-tuple-element.129) | copy-start | bytes 52
  25.9 7.9 %copy-start.41 = (pred[16]{0:T(512)(128)(4,1)}, pred[16]{0:T(512)(128)(4,1)S(1)}, u32[]{:S(2)}) copy-start(pred[16]{0:T(512)(128)(4,1)S(1)} %get-tuple-element.127) | copy-start | bytes 52
  25.9 13.5 %copy-start.31 = (pred[16]{0:T(512)(128)(4,1)}, pred[16]{0:T(512)(128)(4,1)S(1)}, u32[]{:S(2)}) copy-start(pred[16]{0:T(512)(128)(4,1)S(1)} %get-tuple-element.135) | copy-start | bytes 52
  25.9 13.5 %copy-start.33 = (pred[16]{0:T(512)(128)(4,1)}, pred[16]{0:T(512)(128)(4,1)S(1)}, u32[]{:S(2)}) copy-start(pred[16]{0:T(512)(128)(4,1)S(1)} %get-tuple-element.137) | copy-start | bytes 52
  25.9 7.2 %copy-start.22 = (s32[1024]{0:T(1024)}, s32[1024]{0:T(1024)S(1)}, u32[]{:S(2)}) copy-start(s32[1024]{0:T(1024)S(1)} %pad_clamp_fusion.1) | copy-start | bytes 12292
  26.0 4.6 %copy-start.23 = (s32[1024]{0:T(1024)}, s32[1024]{0:T(1024)S(1)}, u32[]{:S(2)}) copy-start(s32[1024]{0:T(1024)S(1)} %pad_clamp_fusion.2) | copy-start | bytes 12292
  26.0 5.2 %copy-start.24 = (s32[1024]{0:T(1024)}, s32[1024]{0:T(1024)S(1)}, u32[]{:S(2)}) copy-start(s32[1024]{0:T(1024)S(1)} %pad_clamp_fusion.3) | copy-start | bytes 12292
  26.0 5.7 %copy-start.25 = (s32[1024]{0:T(1024)}, s32[1024]{0:T(1024)S(1)}, u32[]{:S(2)}) copy-start(s32[1024]{0:T(1024)S(1)} %pad_clamp_fusion.4) | copy-start | bytes 12292
  26.0 7.1 %copy-start.26 = (s32[1024]{0:T(1024)}, s32[1024]{0:T(1024)S(1)}, u32[]{:S(2)}) copy-start(s32[1024]{0:T(1024)S(1)} %pad_clamp_fusion.5) | copy-start | bytes 12292
  26.1 14.0 %copy-start.27 = (s32[1024]{0:T(1024)}, s32[1024]{0:T(1024)S(1)}, u32[]{:S(2)}) copy-start(s32[1024]{0:T(1024)S(1)} %pad_clamp_fusion.6) | copy-start | bytes 12292
  26.2 3.1 %collective-permute-start.2 = (bf16[6,1,3,128]{3,1,2,0:T(2,128)(2,1)S(1)}, bf16[6,1,3,128]{3,1,2,0:T(2,128)(2,1)S(1)}, u32[]{:S(2)}, u32[]{:S(2)}) collective-permute-start(bf16[6,1,3,128]{3,1,2,0:T(2,128)(2,1)S(1)} %get-tuple-element.121), channel_id=1, source_target_pairs={{0,1},{1,2},{2,3},{3,0},{4,5},{5,6},{6,7},{7,4},{8,9},{9,10},{10,1... | collective-permute-start | bytes 13832 | tf_op jit(solution)/shard_map/ppermute | solution.py:15
  26.2 3.1 %collective-permute-start.3 = (bf16[6,1,3,128]{3,1,2,0:T(2,128)(2,1)S(1)}, bf16[6,1,3,128]{3,1,2,0:T(2,128)(2,1)S(1)}, u32[]{:S(2)}, u32[]{:S(2)}) collective-permute-start(bf16[6,1,3,128]{3,1,2,0:T(2,128)(2,1)S(1)} %get-tuple-element.122), channel_id=1, source_target_pairs={{1,0},{2,1},{3,2},{0,3},{5,4},{6,5},{7,6},{4,7},{9,8},{10,9},{11,1... | collective-permute-start | bytes 13832 | tf_op jit(solution)/shard_map/ppermute | solution.py:16
  28.0 18.0 %copy-start.28 = (s32[1024]{0:T(1024)}, s32[1024]{0:T(1024)S(1)}, u32[]{:S(2)}) copy-start(s32[1024]{0:T(1024)S(1)} %pad_clamp_fusion.7) | copy-start | bytes 12292
  36.4 9.6 %copy-start.2 = (bf16[1,4,128,256]{3,2,1,0:T(8,128)(2,1)}, bf16[1,4,128,256]{3,2,1,0:T(8,128)(2,1)S(1)}, u32[]{:S(2)}) copy-start(bf16[1,4,128,256]{3,2,1,0:T(8,128)(2,1)S(1)} %collective-permute-done.4) | copy-start | bytes 786436
  36.5 9.5 %copy-start.3 = (bf16[1,4,128,256]{3,2,1,0:T(8,128)(2,1)}, bf16[1,4,128,256]{3,2,1,0:T(8,128)(2,1)S(1)}, u32[]{:S(2)}) copy-start(bf16[1,4,128,256]{3,2,1,0:T(8,128)(2,1)S(1)} %collective-permute-done.5) | copy-start | bytes 786436
  36.6 9.4 %collective-permute-start.6 = (bf16[6,1,128,256]{3,2,1,0:T(8,128)(2,1)S(1)}, bf16[6,1,128,256]{3,2,1,0:T(8,128)(2,1)S(1)}, u32[]{:S(2)}, u32[]{:S(2)}) collective-permute-start(bf16[6,1,128,256]{3,2,1,0:T(8,128)(2,1)S(1)} %get-tuple-element.84), channel_id=1, source_target_pairs={{0,1},{1,2},{2,3},{3,0},{4,5},{5,6},{6,7},{7,4},{8,9},{9,10},{10,1... | collective-permute-start | bytes 1179656 | tf_op jit(solution)/shard_map/ppermute | solution.py:15
  38.3 8.9 %collective-permute-start.7 = (bf16[6,1,128,256]{3,2,1,0:T(8,128)(2,1)S(1)}, bf16[6,1,128,256]{3,2,1,0:T(8,128)(2,1)S(1)}, u32[]{:S(2)}, u32[]{:S(2)}) collective-permute-start(bf16[6,1,128,256]{3,2,1,0:T(8,128)(2,1)S(1)} %get-tuple-element.85), channel_id=1, source_target_pairs={{1,0},{2,1},{3,2},{0,3},{5,4},{6,5},{7,6},{4,7},{9,8},{10,9},{11,1... | collective-permute-start | bytes 1179656 | tf_op jit(solution)/shard_map/ppermute | solution.py:16
  57.8 3.6 %copy-start.44 = (pred[16]{0:T(512)(128)(4,1)S(1)}, pred[16]{0:T(512)(128)(4,1)}, u32[]{:S(2)}) copy-start(pred[16]{0:T(512)(128)(4,1)} %copy-done.43) | copy-start | bytes 52
  61.3 2.4 %copy-start.9 = (bf16[16,128,256]{2,1,0:T(8,128)(2,1)S(1)}, bf16[16,128,256]{2,1,0:T(8,128)(2,1)}, u32[]{:S(2)}) copy-start(bf16[16,128,256]{2,1,0:T(8,128)(2,1)} %gather_fusion.11) | copy-start | bytes 3145732
  61.3 2.4 %copy-start.42 = (pred[16]{0:T(512)(128)(4,1)S(1)}, pred[16]{0:T(512)(128)(4,1)}, u32[]{:S(2)}) copy-start(pred[16]{0:T(512)(128)(4,1)} %copy-done.41) | copy-start | bytes 52
  63.8 1.7 copy-start.8
  63.8 1.7 copy-start.40
  65.5 1.7 copy-start.7
  65.6 1.7 copy-start.11
  65.6 1.7 copy-start.38
  67.3 1.8 copy-start.6
  67.3 1.8 copy-start.12
  67.3 1.8 copy-start.13
  67.3 1.8 copy-start.14
  67.3 1.8 copy-start.36
  69.1 1.8 copy-start.5
  69.1 1.8 copy-start.18
  69.1 1.8 copy-start.19
  69.1 1.8 copy-start.20
  69.1 1.8 copy-start.34
  70.9 1.8 copy-start.4
  70.9 1.8 copy-start.15
  70.9 1.8 copy-start.16
  70.9 1.8 copy-start.17
  70.9 1.8 copy-start.32
  72.7 1.7 copy-start.30
  160.6 61.3 %copy-start = (f32[2048,256]{0,1:T(8,128)S(1)}, f32[2048,256]{0,1:T(8,128)}, u32[]{:S(2)}) copy-start(f32[2048,256]{0,1:T(8,128)} %copy.36) | copy-start | bytes 6291460
Sparse Core Ops, SparseCore 0:
  81.4 75.1 all-gather.2
